TPU v7x, 32 devices: a whole 2x2x4 slice. The times are simulated.
32 devices in a mesh: head: 2 (over x), blk: 16 (over z, y, core).
Axes of the slice: x: 2, y: 2, z: 4, core: 2. Of those that a mesh axis runs over, the one named last changes fastest.
Arguments:
- query_rows: bfloat16 [512, 1536], P(('head', 'blk')), may hold values from -400 to 400
- key_rows: bfloat16 [512, 1536], P(('head', 'blk')), may hold values from -400 to 400
- value_rows: bfloat16 [512, 1536], P(('head', 'blk')), may hold values from -6 to 6
- residual: bfloat16 [512, 1536], P(('head', 'blk')), may hold values from -6 to 6
- out_weight: bfloat16 [1536, 1536], P('head'), may hold values from -0.15625 to 0.15625
- attention_gate: float32 [1536], replicated, may hold values from 0.5 to 1.5
- norm_shift: float32 [1536], replicated, may hold values from -1 to 1
- norm_scale: float32 [1536], replicated, may hold values from -0.5 to 0.5
- expert_gate: float32 [1536], replicated, may hold values from 0.5 to 1.5
- expert_up: bfloat16 [16, 1536, 4096], P('blk', None, 'head'), may hold values from -0.15625 to 0.15625
- expert_down: bfloat16 [16, 4096, 1536], P('blk', 'head'), may hold values from -0.09375 to 0.09375
- routing: int32 [512, 2], P(('head', 'blk')), may hold values from 0 to 15, as said below
- combine_weight: float32 [512, 2], P(('head', 'blk')), may hold values from 0.2 to 1
Outputs:
- mixed: bfloat16 [512, 1536], P(('head', 'blk'))
Inputs may be any that keep to these rules, and one draw needn't show every extreme that they name: `routing`: the two choices of a token differ. Within the 16 tokens of one device every expert is named at most 2 times, and one expert, the same for every device, is named exactly 2 times by every device.
All inputs are finite; a program needn't handle non-finite values.
Results may differ from a plain program's by a relative error of at most 0.011.
Values may be sent and summed in bfloat16 or wider, within the bound.
A program may use at most 64 MiB of HBM per device.

v0:
```python
import math

import jax
import jax.numpy as jnp
from jax import lax
from jax.sharding import PartitionSpec as P

HD = 64
TOPK = 2


def on_device(
    query_rows,
    key_rows,
    value_rows,
    residual,
    out_weight,
    attention_gate,
    norm_shift,
    norm_scale,
    expert_gate,
    expert_up,
    expert_down,
    routing,
    combine_weight,
):
    tok_rows = query_rows.shape[0]
    model_width = query_rows.shape[1]
    block_count = lax.axis_size("blk")
    cap_slots = max(2, TOPK * tok_rows // block_count)
    query_heads, key_heads, value_heads = (
        lax.all_to_all(query_rows, "head", split_axis=1, concat_axis=0, tiled=True),
        lax.all_to_all(key_rows, "head", split_axis=1, concat_axis=0, tiled=True),
        lax.all_to_all(value_rows, "head", split_axis=1, concat_axis=0, tiled=True),
    )
    head_rows = query_heads.shape[0]
    head_cols = query_heads.shape[1]
    heads_here = head_cols // HD
    score_scale = 1.0 / math.sqrt(HD)
    query_split = query_heads.reshape(head_rows, heads_here, HD)
    peak_old = jnp.full((heads_here, head_rows), -1e30, jnp.float32)
    key_piece = lax.all_gather(key_heads, "blk", axis=0, tiled=True)
    value_piece = lax.all_gather(value_heads, "blk", axis=0, tiled=True)
    piece_rows = key_piece.shape[0]
    key_split = key_piece.reshape(piece_rows, heads_here, HD)
    value_split = value_piece.reshape(piece_rows, heads_here, HD)
    scores = (
        jnp.einsum("rhd,phd->hrp", query_split, key_split, preferred_element_type=jnp.float32)
        * score_scale
    )
    peak_new = jnp.maximum(peak_old, jnp.max(scores, axis=2))
    weights = jnp.exp(scores - peak_new[:, :, None])
    total_new = jnp.sum(weights, axis=2)
    accum_new = jnp.einsum(
        "hrp,phd->hrd",
        weights.astype(jnp.bfloat16),
        value_split,
        preferred_element_type=jnp.float32,
    )
    attended = (
        jnp.transpose(accum_new / total_new[:, :, None], (1, 0, 2))
        .reshape(head_rows, head_cols)
        .astype(jnp.bfloat16)
    )
    projected = lax.psum_scatter(
        jnp.dot(attended, out_weight, preferred_element_type=jnp.float32).astype(jnp.bfloat16),
        "head",
        scatter_dimension=0,
        tiled=True,
    ).astype(jnp.float32)
    middle = residual.astype(jnp.float32) + attention_gate * projected
    average = jnp.mean(middle, axis=1, keepdims=True)
    centered = middle - average
    variance = jnp.mean(centered * centered, axis=1, keepdims=True)
    normed = (centered * lax.rsqrt(variance + 1e-06) * (1.0 + norm_scale) + norm_shift).astype(
        jnp.bfloat16
    )
    flat_choice = routing.reshape(-1)
    onehot = (flat_choice[:, None] == jnp.arange(block_count, dtype=jnp.int32)[None, :]).astype(
        jnp.int32
    )
    earlier = jnp.cumsum(onehot, axis=0) - onehot
    slot_index = flat_choice * cap_slots + jnp.sum(earlier * onehot, axis=1)
    source_rows = jnp.repeat(normed, TOPK, axis=0)
    send_buffer = (
        jnp.zeros((block_count * cap_slots, model_width), jnp.bfloat16)
        .at[slot_index]
        .set(source_rows)
    )
    arrived = lax.all_to_all(send_buffer, "blk", split_axis=0, concat_axis=0, tiled=True)
    hidden = jax.nn.gelu(
        jnp.dot(
            lax.all_gather(arrived, "head", axis=0, tiled=True),
            expert_up[0],
            preferred_element_type=jnp.float32,
        ),
        approximate=True,
    ).astype(jnp.bfloat16)
    partial_sum = lax.psum_scatter(
        jnp.dot(hidden, expert_down[0], preferred_element_type=jnp.float32).astype(jnp.bfloat16),
        "head",
        scatter_dimension=0,
        tiled=True,
    )
    returned_rows = lax.all_to_all(partial_sum, "blk", split_axis=0, concat_axis=0, tiled=True)
    picked = returned_rows[slot_index].reshape(tok_rows, TOPK, model_width).astype(jnp.float32)
    mixture = jnp.sum(picked * combine_weight[:, :, None], axis=1)
    return (middle + expert_gate * mixture).astype(jnp.bfloat16)


def solution(mesh):
    in_specs = (
        P(("head", "blk"), None),
        P(("head", "blk"), None),
        P(("head", "blk"), None),
        P(("head", "blk"), None),
        P("head", None),
        P(),
        P(),
        P(),
        P(),
        P("blk", None, "head"),
        P("blk", "head", None),
        P(("head", "blk"), None),
        P(("head", "blk"), None),
    )
    out_specs = P(("head", "blk"), None)
    return jax.shard_map(
        on_device, mesh=mesh, in_specs=in_specs, out_specs=out_specs, check_vma=False
    )
```

profile of v0, /device:TPU:0, one launch (start us, length us, event | category | flops | bytes accessed | tf_op | source)
XLA Modules:
  0.0 149.9 jit_solution(11957279712682442509)
XLA Ops:
  6.5 1.6 %copy.58 = bf16[2,2,8,768]{3,2,0,1:T(8,128)(2,1)} copy(bf16[2,2,8,768]{3,2,1,0:T(8,128)(2,1)} %bitcast.58) | data formatting | bytes 98304 | tf_op jit(solution)/shard_map/all_to_all | solution.py:33
  8.1 4.2 %all-to-all-start.1 = ((bf16[16,2,768]{2,0,1:T(8,128)(2,1)}), bf16[16,2,768]{2,0,1:T(8,128)(2,1)S(1)}, u32[]{:S(2)}, u32[]{:S(2)}) async-start(bf16[16,2,768]{2,0,1:T(8,128)(2,1)} %bitcast.51), calls=%async_computation.1 | async-start | bytes 98304 | tf_op jit(solution)/shard_map/all_to_all | solution.py:33
  12.3 0.8 copy.45
  13.1 0.7 broadcast_multiply_fusion
  13.7 0.7 broadcast_add_fusion
  14.8 1.4 copy.59
  16.3 1.4 copy.57
  17.9 3.4 %all-to-all-start = ((bf16[16,2,768]{2,0,1:T(8,128)(2,1)}), bf16[16,2,768]{2,0,1:T(8,128)(2,1)S(1)}, u32[]{:S(2)}, u32[]{:S(2)}) async-start(bf16[16,2,768]{2,0,1:T(8,128)(2,1)} %bitcast.52), calls=%async_computation | async-start | bytes 98304 | tf_op jit(solution)/shard_map/all_to_all | solution.py:32
  21.3 25.8 %all_gather.9 = bf16[512,768]{1,0:T(8,128)(2,1)} all-gather(bf16[32,768]{1,0:T(8,128)(2,1)S(1)} %bitcast.55), channel_id=1, replica_groups=mesh['head'=2,'blk'=16] {'blk'}, dimensions={0}, use_global_device_ids=true | all-gather | bytes 835584 | tf_op jit(solution)/shard_map/all_gather | solution.py:42
  47.1 1.4 copy.39
  48.6 3.4 %all-to-all-start.2 = ((bf16[16,2,768]{2,0,1:T(8,128)(2,1)}), bf16[16,2,768]{2,0,1:T(8,128)(2,1)S(1)}, u32[]{:S(2)}, u32[]{:S(2)}) async-start(bf16[16,2,768]{2,0,1:T(8,128)(2,1)} %bitcast.50), calls=%async_computation.2 | async-start | bytes 98304 | tf_op jit(solution)/shard_map/all_to_all | solution.py:34
  52.1 1.2 fusion.41
  53.3 2.7 %all-to-all-done.2 = bf16[16,2,768]{2,0,1:T(8,128)(2,1)S(1)} async-done(((bf16[16,2,768]{2,0,1:T(8,128)(2,1)}), bf16[16,2,768]{2,0,1:T(8,128)(2,1)S(1)}, u32[]{:S(2)}, u32[]{:S(2)}) %all-to-all-start.2) | async-done | bytes 49184 | tf_op jit(solution)/shard_map/all_to_all | solution.py:34
  56.0 19.7 %all_gather.10 = bf16[512,768]{1,0:T(8,128)(2,1)S(1)} all-gather(bf16[32,768]{1,0:T(8,128)(2,1)S(1)} %bitcast.56), channel_id=1, replica_groups=mesh['head'=2,'blk'=16] {'blk'}, dimensions={0}, use_global_device_ids=true | all-gather | bytes 835584 | tf_op jit(solution)/shard_map/all_gather | solution.py:43
  75.7 1.2 copy.42
  76.8 1.4 fusion.9
  78.3 1.8 %fusion.8 = bf16[32,12,64]{2,0,1:T(8,128)(2,1)S(1)} fusion(bf16[512,12,64]{0,2,1:T(8,128)(2,1)} %bitcast.54, f32[12,32,512]{2,1,0:T(8,128)} %get-tuple-element.6, f32[12,32]{1,0:T(8,128)S(1)} %broadcast_maximum_fusion, f32[32,12]{0,1:T(8,128)S(1)} %bitcast.61), kind=kOutput, calls=%fused_computation.11 | convolution fusion | flops 25608192 | bytes 1625088 | tf_op jit(solution)/shard_map/hrp,phd->hrd/dot_general | solution.py:54
  80.2 1.1 convolution_convert_fusion
  81.4 7.7 %reduce-scatter.3.cloned.1.call-done = bf16[16,1536]{1,0:T(8,128)(2,1)} async-done(((bf16[32,1536]{1,0:T(8,128)(2,1)}), bf16[16,1536]{1,0:T(8,128)(2,1)}) %reduce-scatter.3.cloned.1.call-update) | async-done | bytes 49168 | tf_op jit(solution)/shard_map/reduce_scatter | solution.py:65
  89.1 0.9 fusion.32
  90.0 1.0 multiply_reduce_fusion.1
  91.1 0.9 add_convert_fusion.1
  92.1 0.8 scatter_custom_fusion
  92.9 12.8 %all_to_all.78 = bf16[16,2,1536]{2,1,0:T(2,128)(2,1)S(1)} all-to-all(bf16[16,2,1536]{2,1,0:T(2,128)(2,1)S(1)} %all_to_all.67), channel_id=1, replica_groups=mesh['head'=2,'blk'=16] {'blk'}, dimensions={0} | all-to-all | bytes 196608 | tf_op jit(solution)/shard_map/all_to_all | solution.py:90
  105.8 5.3 %all_gather.11 = bf16[64,1536]{1,0:T(8,128)(2,1)S(1)} all-gather(bf16[32,1536]{1,0:T(8,128)(2,1)S(1)} %all_to_all.69), channel_id=1, replica_groups=mesh['head'=2,'blk'=16] {'head'}, dimensions={0}, use_global_device_ids=true | all-gather | bytes 294912 | tf_op jit(solution)/shard_map/all_gather | solution.py:93
  111.1 7.7 %fusion.4 = bf16[64,1536]{1,0:T(8,128)(2,1)} fusion(bf16[1,2048,1536]{2,1,0:T(8,128)(2,1)} %param.23, bf16[64,1536]{1,0:T(8,128)(2,1)S(1)} %all_gather.11, bf16[1,1536,2048]{2,1,0:T(8,128)(2,1)} %param.22), kind=kOutput, calls=%fused_computation.6 | convolution fusion | flops 806584320 | bytes 12976128 | tf_op jit(solution)/shard_map/dot_general | solution.py:100
  118.8 7.9 %reduce-scatter.5.cloned.1.call-done = bf16[32,1536]{1,0:T(8,128)(2,1)} async-done(((bf16[64,1536]{1,0:T(8,128)(2,1)}), bf16[32,1536]{1,0:T(8,128)(2,1)}) %reduce-scatter.5.cloned.1.call-update) | async-done | bytes 98320 | tf_op jit(solution)/shard_map/reduce_scatter | solution.py:99
  126.6 1.6 %all_to_all.70 = bf16[16,2,1536]{2,1,0:T(2,128)(2,1)} reshape(bf16[32,1536]{1,0:T(8,128)(2,1)} %reduce-scatter.5.cloned.1.call-done) | data formatting | bytes 196608 | tf_op jit(solution)/shard_map/all_to_all | solution.py:105
  128.2 5.6 %all-to-all-start.4 = ((bf16[16,2,1536]{2,1,0:T(2,128)(2,1)}), bf16[16,2,1536]{2,1,0:T(2,128)(2,1)S(1)}, u32[]{:S(2)}, u32[]{:S(2)}) async-start(bf16[16,2,1536]{2,1,0:T(2,128)(2,1)} %all_to_all.70), calls=%async_computation.6 | async-start | bytes 196608 | tf_op jit(solution)/shard_map/all_to_all | solution.py:105
  133.9 7.3 %all-to-all-done.4 = bf16[16,2,1536]{2,1,0:T(2,128)(2,1)S(1)} async-done(((bf16[16,2,1536]{2,1,0:T(2,128)(2,1)}), bf16[16,2,1536]{2,1,0:T(2,128)(2,1)S(1)}, u32[]{:S(2)}, u32[]{:S(2)}) %all-to-all-start.4) | async-done | bytes 98336 | tf_op jit(solution)/shard_map/all_to_all | solution.py:105
  141.3 0.6 gather_fusion
  142.4 0.6 add_convert_fusion
  (42 shorter events, 1.8 us)
Async XLA Ops:
  6.5 73.7 %copy-start = (bf16[768,1536]{1,0:T(8,128)(2,1)S(1)}, bf16[768,1536]{1,0:T(8,128)(2,1)}, u32[]{:S(2)}) copy-start(bf16[768,1536]{1,0:T(8,128)(2,1)} %param.17) | copy-start | bytes 7077892
  8.1 9.8 %all-to-all-start.1 = ((bf16[16,2,768]{2,0,1:T(8,128)(2,1)}), bf16[16,2,768]{2,0,1:T(8,128)(2,1)S(1)}, u32[]{:S(2)}, u32[]{:S(2)}) async-start(bf16[16,2,768]{2,0,1:T(8,128)(2,1)} %bitcast.51), calls=%async_computation.1 | async-start | bytes 98304 | tf_op jit(solution)/shard_map/all_to_all | solution.py:33
  17.9 71.2 %copy-start.1 = (bf16[16,1536]{1,0:T(8,128)(2,1)S(1)}, bf16[16,1536]{1,0:T(8,128)(2,1)}, u32[]{:S(2)}) copy-start(bf16[16,1536]{1,0:T(8,128)(2,1)} %param.16) | copy-start | bytes 147460
  17.9 71.2 %copy-start.3 = (f32[1536]{0:T(1024)S(1)}, f32[1536]{0:T(1024)}, u32[]{:S(2)}) copy-start(f32[1536]{0:T(1024)} %param.18) | copy-start | bytes 18436
  17.9 30.7 %all-to-all-start = ((bf16[16,2,768]{2,0,1:T(8,128)(2,1)}), bf16[16,2,768]{2,0,1:T(8,128)(2,1)S(1)}, u32[]{:S(2)}, u32[]{:S(2)}) async-start(bf16[16,2,768]{2,0,1:T(8,128)(2,1)} %bitcast.52), calls=%async_computation | async-start | bytes 98304 | tf_op jit(solution)/shard_map/all_to_all | solution.py:32
  21.3 69.7 %copy-start.5 = (f32[1536]{0:T(1024)S(1)}, f32[1536]{0:T(1024)}, u32[]{:S(2)}) copy-start(f32[1536]{0:T(1024)} %param.19) | copy-start | bytes 18436
  48.6 7.4 %all-to-all-start.2 = ((bf16[16,2,768]{2,0,1:T(8,128)(2,1)}), bf16[16,2,768]{2,0,1:T(8,128)(2,1)S(1)}, u32[]{:S(2)}, u32[]{:S(2)}) async-start(bf16[16,2,768]{2,0,1:T(8,128)(2,1)} %bitcast.50), calls=%async_computation.2 | async-start | bytes 98304 | tf_op jit(solution)/shard_map/all_to_all | solution.py:34
  52.0 37.1 %reduce-scatter.3.cloned.1.call-start = ((), (), s32[]{:S(2)}) async-start(), calls=%async_computation.7 | async-start | bytes 147456 | tf_op jit(solution)/shard_map/reduce_scatter | solution.py:65
  81.4 45.2 %reduce-scatter.5.cloned.1.call-start = ((), (), s32[]{:S(2)}) async-start(), calls=%async_computation.8 | async-start | bytes 294912 | tf_op jit(solution)/shard_map/reduce_scatter | solution.py:99
  111.1 22.8 %copy-start.6 = (f32[16,2]{0,1:T(2,128)S(1)}, f32[16,2]{0,1:T(2,128)}, u32[]{:S(2)}) copy-start(f32[16,2]{0,1:T(2,128)} %param.25) | copy-start | bytes 388
  111.1 31.3 %copy-start.2 = (bf16[16,1536]{1,0:T(8,128)(2,1)S(1)}, bf16[16,1536]{1,0:T(8,128)(2,1)}, u32[]{:S(2)}) copy-start(bf16[16,1536]{1,0:T(8,128)(2,1)} %reduce-scatter.3.cloned.1.call-done) | copy-start | bytes 147460
  111.1 31.3 %copy-start.4 = (f32[1536]{0:T(1024)S(1)}, f32[1536]{0:T(1024)}, u32[]{:S(2)}) copy-start(f32[1536]{0:T(1024)} %param.21) | copy-start | bytes 18436
  128.2 13.0 %all-to-all-start.4 = ((bf16[16,2,1536]{2,1,0:T(2,128)(2,1)}), bf16[16,2,1536]{2,1,0:T(2,128)(2,1)S(1)}, u32[]{:S(2)}, u32[]{:S(2)}) async-start(bf16[16,2,1536]{2,1,0:T(2,128)(2,1)} %all_to_all.70), calls=%async_computation.6 | async-start | bytes 196608 | tf_op jit(solution)/shard_map/all_to_all | solution.py:105
Sparse Core Ops, SparseCore 0:
  81.5 7.5 reduce-scatter.2
  118.9 7.7 reduce-scatter.4
where the time goes:
time: 151 us; the launch traced here: 150 us
  blocking collectives  63.6 us (42%)
  waiting for transfers between devices  25.6 us (17%)
  starting transfers between devices  16.7 us (11%)
  between operations  13.6 us (9%)
  local copies, waits for them, and re-layouts  11.7 us (8%)
  matrix products  11.7 us (8%)
  other arithmetic  6.89 us (5%)
    all_gather x1, blocking collectives, on_device(): key_piece = lax.all_gather(key_heads, 'blk', axis=0, tiled=True)  25.8 us
    all_gather x1, blocking collectives, on_device(): value_piece = lax.all_gather(value_heads, 'blk', axis=0, tiled=True)  19.7 us
    all_to_all x1, blocking collectives, on_device(): lax.all_to_all(send_buffer, 'blk', split_axis=0, concat_axis=0, tiled=True)  12.8 us
    reduce_scatter x1, waiting for transfers between devices, on_device(): lax.psum_scatter(jnp.dot(hidden, expert_down[0], preferred_element_type=j...  7.87 us
    dot_general x1, matrix products, on_device(): jnp.dot(hidden, expert_down[0], preferred_element_type=jnp.float32)  7.67 us
    reduce_scatter x1, waiting for transfers between devices, on_device(): lax.psum_scatter(jnp.dot(attended, out_weight, preferred_element_type=jnp...  7.65 us
    all_to_all x1, waiting for transfers between devices, on_device(): lax.all_to_all(partial_sum, 'blk', split_axis=0, concat_axis=0, tiled=True)  7.31 us
    all_to_all x1, starting transfers between devices, on_device(): lax.all_to_all(partial_sum, 'blk', split_axis=0, concat_axis=0, tiled=True)  5.62 us
  transfers between devices with their start and end apart: 6, of which 4 were waited for; matrix products, arithmetic and copies ran while one was open for 6% of the time, Pallas kernels for 0%

commit v1 on v0

v1 whole, which is shorter than its diff:
```python
import functools
import math

import jax
import jax.numpy as jnp
from jax import lax
from jax.experimental import pallas as pl
from jax.experimental.pallas import tpu as pltpu
from jax.sharding import PartitionSpec as P

HD = 64
TOPK = 2
LANES = 128
MESH = pl.DeviceIdType.MESH
F32 = jnp.float32
BF16 = jnp.bfloat16


def round_up(value, step):
    return -(-value // step) * step


def dot(left, right):
    return lax.dot_general(left, right, (((1,), (0,)), ((), ())), preferred_element_type=F32)


def dot_nt(left, right):
    return lax.dot_general(left, right, (((1,), (1,)), ((), ())), preferred_element_type=F32)


def dot_tn(left, right):
    return lax.dot_general(left, right, (((0,), (0,)), ((), ())), preferred_element_type=F32)


def wait_bytes(ref, sem):
    pltpu.make_async_copy(ref, ref, sem).wait()


def kernel(
    dims,
    q_ref, k_ref, v_ref, res_ref, ag_ref, shift_ref, scale_ref, eg_ref, route_ref, comb_ref,
    ow_hbm, up_hbm, down_hbm,
    out_ref,
    ow, up, down,
    kvs, kvr, qs, qr, ats, atr, ps, pr, sb, xr, eb, rr,
    mid, wide, thin, hidden, flat,
    wsem, ssem, rsem,
):
    nh, nb, sub, cap = dims
    n = nh * nb
    quarter = nb // sub
    tok, width = q_ref.shape
    gcols = width // (nh * sub)
    heads = gcols // HD
    win = qs.shape[2]
    kvcols = kvs.shape[2]
    klo = kvcols - win
    pieces = width // LANES
    h = lax.axis_index("head")
    b = lax.axis_index("blk")
    me = h * nb + b
    k_own = b // quarter
    m_own = lax.rem(b, quarter)

    fetch = [
        pltpu.make_async_copy(ow_hbm, ow, wsem.at[0]),
        pltpu.make_async_copy(up_hbm.at[0], up, wsem.at[1]),
        pltpu.make_async_copy(down_hbm.at[0], down, wsem.at[2]),
    ]
    for copy in fetch:
        copy.start()

    barrier = pltpu.get_barrier_semaphore()

    def greet(step, carry):
        to = lax.rem(me + step, n)
        pl.semaphore_signal(
            barrier, inc=1, device_id=(to // nb, lax.rem(to, nb)), device_id_type=MESH
        )
        return carry

    lax.fori_loop(1, n, greet, 0)

    for g in range(nh * sub):
        cols = slice(g * gcols, (g + 1) * gcols)
        kvs[g, :, 0:gcols] = v_ref[:, cols]
        kvs[g, :, kvcols - gcols:kvcols] = k_ref[:, cols]
        if kvcols > 2 * gcols:
            kvs[g, :, gcols:kvcols - gcols] = jnp.zeros((tok, kvcols - 2 * gcols), BF16)
        if win > gcols:
            qs[g, :, 0:win - gcols] = jnp.zeros((tok, win - gcols), BF16)
        qs[g, :, win - gcols:win] = q_ref[:, cols]

    pl.semaphore_wait(barrier, n - 1)

    def remote(src, dst, phase, to_h, to_b):
        pltpu.make_async_remote_copy(
            src_ref=src, dst_ref=dst, send_sem=ssem.at[phase], recv_sem=rsem.at[phase],
            device_id=(to_h, to_b), device_id_type=MESH,
        ).start()

    def local(src, dst, phase):
        pltpu.make_async_copy(src, dst, rsem.at[phase]).start()

    def send_q(step, carry):
        group = lax.rem(h * sub + k_own + step, nh * sub)
        to_h, to_s = group // sub, lax.rem(group, sub)
        remote(qs.at[group], qr.at[k_own * nh + h], 1, to_h, to_s * quarter + m_own)
        return carry

    lax.fori_loop(1, nh * sub, send_q, 0)
    local(qs.at[h * sub + k_own], qr.at[k_own * nh + h], 1)

    def send_kv(step, carry):
        to = lax.rem(me + step, n)
        to_h, to_b = to // nb, lax.rem(to, nb)
        remote(kvs.at[to_h * sub + to_b // quarter], kvr.at[me], 0, to_h, to_b)
        return carry

    lax.fori_loop(1, n, send_kv, 0)
    local(kvs.at[h * sub + k_own], kvr.at[me], 0)

    slots = nb * cap
    row = lax.broadcasted_iota(jnp.int32, (slots, tok), 0)
    expert = row // cap
    place = (row - expert * cap).astype(F32)
    first = route_ref[0:1, :] == expert
    second = route_ref[1:2, :] == expert
    named = jnp.where(first | second, 1.0, 0.0)
    tri = jnp.where(
        lax.broadcasted_iota(jnp.int32, (tok, tok), 0) < lax.broadcasted_iota(jnp.int32, (tok, tok), 1),
        1.0, 0.0,
    )
    earlier = dot(named.astype(BF16), tri.astype(BF16))
    here = earlier == place
    pick = [jnp.where(choice & here, 1.0, 0.0) for choice in (first, second)]
    eye = lax.broadcasted_iota(jnp.int32, (tok, tok), 0) == lax.broadcasted_iota(jnp.int32, (tok, tok), 1)

    wait_bytes(qr, rsem.at[1])
    wait_bytes(kvr, rsem.at[0])

    rows = nh * sub * tok
    queries = qr[...].reshape(rows, win)
    keys = kvr[:, :, klo:kvcols].reshape(n * tok, win)
    values = kvr[:, :, 0:win].reshape(n * tok, win)
    lane = lax.broadcasted_iota(jnp.int32, (rows, win), 1)
    attended = jnp.zeros((rows, win), F32)
    for j in range(heads):
        lo = win - gcols + j * HD
        q_j = jnp.where((lane >= lo) & (lane < lo + HD), queries, jnp.zeros_like(queries))
        scores = dot_nt(q_j, keys) * (1.0 / math.sqrt(HD))
        probs = jnp.exp(scores - jnp.max(scores, axis=1, keepdims=True))
        total = jnp.sum(probs, axis=1, keepdims=True)
        numer = dot(probs.astype(BF16), values)
        attended = jnp.where((lane >= j * HD) & (lane < (j + 1) * HD), numer / total, attended)
    ats[...] = attended.astype(BF16).reshape(sub, nh * tok, win)

    def send_att(step, carry):
        to_k = lax.rem(k_own + step, sub)
        remote(ats.at[to_k], atr.at[k_own], 2, h, to_k * quarter + m_own)
        return carry

    lax.fori_loop(1, sub, send_att, 0)
    local(ats.at[k_own], atr.at[k_own], 2)
    fetch[0].wait()
    wait_bytes(atr, rsem.at[2])

    partial = jnp.zeros((nh * tok, width), F32)
    for s in range(sub):
        partial = partial + dot(atr[s, :, 0:gcols], ow[s * gcols:(s + 1) * gcols, :])
    ps[...] = partial.astype(BF16).reshape(nh, tok, width)

    def send_part(step, carry):
        to_h = lax.rem(h + step, nh)
        remote(ps.at[to_h], pr.at[h], 3, to_h, b)
        return carry

    lax.fori_loop(1, nh, send_part, 0)
    local(ps.at[h], pr.at[h], 3)
    wait_bytes(pr, rsem.at[3])

    projected = jnp.sum(pr[...].astype(F32), axis=0)
    middle = res_ref[...].astype(F32) + ag_ref[...] * projected
    average = jnp.mean(middle, axis=1, keepdims=True)
    centered = middle - average
    variance = jnp.mean(centered * centered, axis=1, keepdims=True)
    normed = (
        centered * lax.rsqrt(variance + 1e-06) * (1.0 + scale_ref[...]) + shift_ref[...]
    ).astype(BF16)
    mid[...] = middle

    buffer = dot((pick[0] + pick[1]).astype(BF16), normed)
    for c in range(pieces):
        thin[pl.ds(c, slots, pieces), :] = buffer[:, c * LANES:(c + 1) * LANES]
    sb[...] = thin[...].reshape(sb.shape).astype(BF16)

    def send_rows(step, carry):
        to = lax.rem(me + step, n)
        to_h, to_b = to // nb, lax.rem(to, nb)
        remote(sb.at[to_b], xr.at[me], 4, to_h, to_b)
        return carry

    lax.fori_loop(1, n, send_rows, 0)
    local(sb.at[b], xr.at[me], 4)
    fetch[1].wait()
    wait_bytes(xr, rsem.at[4])

    wide[...] = xr[...].astype(F32).reshape(wide.shape)
    for c in range(pieces):
        flat[:, c * LANES:(c + 1) * LANES] = wide[pl.ds(c, n * cap, pieces), :].astype(BF16)

    ff = up.shape[1]
    up_tile = math.gcd(ff, 512)

    def up_step(i, carry):
        cols = pl.ds(pl.multiple_of(i * up_tile, up_tile), up_tile)
        u = dot(flat[...], up[:, cols])
        inner = math.sqrt(2.0 / math.pi) * (u + 0.044715 * (u * u * u))
        hidden[:, cols] = (0.5 * u * (1.0 + jnp.tanh(inner))).astype(BF16)
        return carry

    lax.fori_loop(0, ff // up_tile, up_step, 0)
    fetch[2].wait()
    down_tile = math.gcd(width, 512)
    for i in range(width // down_tile):
        part = dot(hidden[...], down[:, i * down_tile:(i + 1) * down_tile])
        for c in range(down_tile // LANES):
            wide[pl.ds(i * (down_tile // LANES) + c, n * cap, pieces), :] = part[:, c * LANES:(c + 1) * LANES]
    eb[...] = wide[...].reshape(eb.shape).astype(BF16)

    def send_back(step, carry):
        to = lax.rem(me + step, n)
        remote(eb.at[to], rr.at[me], 5, to // nb, lax.rem(to, nb))
        return carry

    lax.fori_loop(1, n, send_back, 0)
    local(eb.at[me], rr.at[me], 5)

    wait_bytes(kvr.at[pl.ds(0, n - 1)], ssem.at[0])
    wait_bytes(qr.at[pl.ds(0, nh * sub - 1)], ssem.at[1])
    if sub > 1:
        wait_bytes(atr.at[pl.ds(0, sub - 1)], ssem.at[2])
    wait_bytes(pr.at[pl.ds(0, nh - 1)], ssem.at[3])
    wait_bytes(xr.at[pl.ds(0, n - 1)], ssem.at[4])

    wait_bytes(rr, rsem.at[5])
    summed = rr[0:nb].astype(F32)
    for other in range(1, nh):
        summed = summed + rr[other * nb:(other + 1) * nb].astype(F32)
    thin[...] = summed.reshape(thin.shape)
    weights = [
        jnp.sum(jnp.where(eye, comb_ref[i:i + 1, :], 0.0), axis=1, keepdims=True) for i in range(TOPK)
    ]
    back = jnp.concatenate(
        [thin[pl.ds(c, slots, pieces), :].astype(BF16) for c in range(pieces)], axis=1
    )
    mixture = weights[0] * dot_tn(pick[0].astype(BF16), back)
    mixture = mixture + weights[1] * dot_tn(pick[1].astype(BF16), back)
    out_ref[...] = (mid[...] + eg_ref[...] * mixture).astype(BF16)
    wait_bytes(rr.at[pl.ds(0, n - 1)], ssem.at[5])


def on_device(
    nh, nb,
    query_rows, key_rows, value_rows, residual, out_weight, attention_gate, norm_shift, norm_scale,
    expert_gate, expert_up, expert_down, routing, combine_weight,
):
    tok, width = query_rows.shape
    n = nh * nb
    cap = max(2, TOPK * tok // nb)
    sub = math.gcd(width // HD // nh, nb)
    gcols = width // (nh * sub)
    win = round_up(gcols, LANES)
    kvcols = round_up(2 * gcols, LANES)
    pieces = width // LANES
    block = cap * pieces
    ff = expert_up.shape[2]
    vmem = pl.BlockSpec(memory_space=pltpu.VMEM)
    anywhere = pl.BlockSpec(memory_space=pl.ANY)
    as_row = lambda vector: vector.reshape(1, width)
    return pl.pallas_call(
        functools.partial(kernel, (nh, nb, sub, cap)),
        out_shape=jax.ShapeDtypeStruct((tok, width), BF16),
        in_specs=[vmem] * 10 + [anywhere] * 3,
        out_specs=vmem,
        scratch_shapes=[
            pltpu.VMEM(out_weight.shape, BF16),
            pltpu.VMEM(expert_up.shape[1:], BF16),
            pltpu.VMEM(expert_down.shape[1:], BF16),
            pltpu.VMEM((nh * sub, tok, kvcols), BF16),
            pltpu.VMEM((n, tok, kvcols), BF16),
            pltpu.VMEM((nh * sub, tok, win), BF16),
            pltpu.VMEM((nh * sub, tok, win), BF16),
            pltpu.VMEM((sub, nh * tok, win), BF16),
            pltpu.VMEM((sub, nh * tok, win), BF16),
            pltpu.VMEM((nh, tok, width), BF16),
            pltpu.VMEM((nh, tok, width), BF16),
            pltpu.VMEM((nb, block, LANES), BF16),
            pltpu.VMEM((n, block, LANES), BF16),
            pltpu.VMEM((n, block, LANES), BF16),
            pltpu.VMEM((n, block, LANES), BF16),
            pltpu.VMEM((tok, width), F32),
            pltpu.VMEM((n * block, LANES), F32),
            pltpu.VMEM((nb * block, LANES), F32),
            pltpu.VMEM((n * cap, ff), BF16),
            pltpu.VMEM((n * cap, width), BF16),
            pltpu.SemaphoreType.DMA((3,)),
            pltpu.SemaphoreType.DMA((6,)),
            pltpu.SemaphoreType.DMA((6,)),
        ],
        compiler_params=pltpu.CompilerParams(
            collective_id=0, has_side_effects=True, vmem_limit_bytes=60 * 1024 * 1024
        ),
        name="layer",
    )(
        query_rows, key_rows, value_rows, residual,
        as_row(attention_gate), as_row(norm_shift), as_row(norm_scale), as_row(expert_gate),
        routing.T, combine_weight.T,
        out_weight, expert_up, expert_down,
    )


def solution(mesh):
    tokens = P(("head", "blk"), None)
    in_specs = (
        tokens, tokens, tokens, tokens,
        P("head", None), P(), P(), P(), P(),
        P("blk", None, "head"), P("blk", "head", None), tokens, tokens,
    )
    return jax.shard_map(
        functools.partial(on_device, mesh.shape["head"], mesh.shape["blk"]),
        mesh=mesh, in_specs=in_specs, out_specs=tokens, check_vma=False,
    )
```

time: 151 us -> 51.1 us (0.34)
  blocking collectives: 63.6 us -> 0 us
  Pallas kernels: 0 us -> 44 us
  waiting for transfers between devices: 25.6 us -> 0 us
  starting transfers between devices: 16.7 us -> 0 us
  between operations: 13.6 us -> 0.01 us
  matrix products: 11.7 us -> 0 us
  other arithmetic: 6.89 us -> 0 us
  local copies, waits for them, and re-layouts: 11.7 us -> 6.59 us
    all_gather x3 -> x0, blocking collectives: 50.8 us -> none  [the longest x1 25.8 us: on_device(): key_piece = lax.all_gather(key_heads, 'blk', axis=0, tiled=True)]
    pallas_call x0 -> x1, Pallas kernels: none -> 44 us  [on_device(): pl.pallas_call(functools.partial(kernel, (nh, nb, sub, cap)), out_shape=j...]
    all_to_all x4 -> x0, starting transfers between devices: 16.7 us -> none  [the longest x1 5.62 us: on_device(): lax.all_to_all(partial_sum, 'blk', split_axis=0, concat_axis=0, tiled=True)]
    reduce_scatter x2 -> x0, waiting for transfers between devices: 15.5 us -> none  [the longest x1 7.87 us: on_device(): lax.psum_scatter(jnp.dot(hidden, expert_down[0], preferred_element_type=j...]
    all_to_all x1 -> x0, blocking collectives: 12.8 us -> none  [on_device(): lax.all_to_all(send_buffer, 'blk', split_axis=0, concat_axis=0, tiled=True)]
    dot_general x4 -> x0, matrix products: 11.7 us -> none  [the longest x1 7.67 us: on_device(): jnp.dot(hidden, expert_down[0], preferred_element_type=jnp.float32)]
    all_to_all x4 -> x0, waiting for transfers between devices: 10 us -> none  [the longest x1 7.31 us: on_device(): lax.all_to_all(partial_sum, 'blk', split_axis=0, concat_axis=0, tiled=True)]
    all_to_all x7 -> x0, local copies, waits for them, and re-layouts: 6.09 us -> none  [the longest x2 1.59 us: on_device(): lax.all_to_all(partial_sum, 'blk', split_axis=0, concat_axis=0, tiled=True)]
  transfers between devices with their start and end apart: 6 -> 0, of which waited for: 4 -> 0; matrix products, arithmetic and copies ran while one was open for 6% -> 0% of each run, Pallas kernels for 0% -> 0%
where the time goes in v1:
time: 51.1 us; the launch traced here: 50.6 us
  Pallas kernels  44 us (86%)
  local copies, waits for them, and re-layouts  6.59 us (13%)
    pallas_call x1, Pallas kernels, on_device(): pl.pallas_call(functools.partial(kernel, (nh, nb, sub, cap)), out_shape=j...  44 us
    reshape x4, local copies, waits for them, and re-layouts, on_device(): as_row = lambda vector: vector.reshape(1, width)  5.17 us
    unnamed x1, local copies, waits for them, and re-layouts  1.42 us

profile of v1, /device:TPU:0, one launch (start us, length us, event | category | flops | bytes accessed | tf_op | source)
XLA Modules:
  0.0 50.6 jit_solution(10541640332934806018)
XLA Ops:
  0.0 1.3 %reshape.12.ag_ref = f32[1,1536]{1,0:T(1,128)} reshape(f32[1536]{0:T(1024)} %param.18) | data formatting | bytes 12288 | tf_op jit(solution)/shard_map/reshape | solution.py:280
  1.3 1.3 %reshape.13.shift_ref = f32[1,1536]{1,0:T(1,128)} reshape(f32[1536]{0:T(1024)} %param.19) | data formatting | bytes 12288 | tf_op jit(solution)/shard_map/reshape | solution.py:280
  2.6 1.3 %reshape.14.scale_ref = f32[1,1536]{1,0:T(1,128)} reshape(f32[1536]{0:T(1024)} %param.20) | data formatting | bytes 12288 | tf_op jit(solution)/shard_map/reshape | solution.py:280
  3.9 1.3 %reshape.15.eg_ref = f32[1,1536]{1,0:T(1,128)} reshape(f32[1536]{0:T(1024)} %param.21) | data formatting | bytes 12288 | tf_op jit(solution)/shard_map/reshape | solution.py:280
  5.2 44.0 %layer.1 = bf16[16,1536]{1,0:T(8,128)(2,1)} custom-call(bf16[16,1536]{1,0:T(8,128)(2,1)} %q_ref.1, bf16[16,1536]{1,0:T(8,128)(2,1)} %k_ref.1, bf16[16,1536]{1,0:T(8,128)(2,1)} %v_ref.1, bf16[16,1536]{1,0:T(8,128)(2,1)} %res_ref.1, f32[1,1536]{1,0:T(1,128)} %reshape.12.ag_ref, f32[1,1536]{1,0:T(1,128)} %reshape.13.shift_ref, f32[1,1536]{1,0:T(1,128)} %reshape.14.scale_ref, ...), custom_call_target="tpu_custom_call" | custom-call | tf_op jit(solution)/shard_map/layer/pallas_call | solution.py:281
  49.2 1.4 %copy.15 = bf16[16,1536]{1,0:T(8,128)(2,1)} copy(bf16[16,1536]{1,0:T(8,128)(2,1)} %layer.1) | data formatting | bytes 98304

commit v2 on v1

--- a/solution.py
+++ b/solution.py
@@ -30,6 +30,10 @@
 
 def dot_tn(left, right):
     return lax.dot_general(left, right, (((0,), (0,)), ((), ())), preferred_element_type=F32)
+
+
+def wrap(index, size):
+    return jnp.where(index >= size, index - size, index)
 
 
 def wait_bytes(ref, sem):
@@ -59,8 +63,11 @@
     h = lax.axis_index("head")
     b = lax.axis_index("blk")
     me = h * nb + b
-    k_own = b // quarter
-    m_own = lax.rem(b, quarter)
+    k_own = lax.div(b, quarter)
+    m_own = b - k_own * quarter
+    side = lax.rem(b, 2)
+    half = n // 2
+    half_me = h * (nb // 2) + lax.div(b, 2)
 
     fetch = [
         pltpu.make_async_copy(ow_hbm, ow, wsem.at[0]),
@@ -72,14 +79,20 @@
 
     barrier = pltpu.get_barrier_semaphore()
 
-    def greet(step, carry):
-        to = lax.rem(me + step, n)
-        pl.semaphore_signal(
-            barrier, inc=1, device_id=(to // nb, lax.rem(to, nb)), device_id_type=MESH
-        )
-        return carry
-
-    lax.fori_loop(1, n, greet, 0)
+    def each_other(act):
+        for far in range(nh):
+            to_h = wrap(h + far, nh)
+
+            def step_to(step, carry, to_h=to_h):
+                act(to_h, wrap(b + step, nb))
+                return carry
+
+            lax.fori_loop(1 if far == 0 else 0, nb, step_to, 0, unroll=nb <= 16)
+
+    def greet(to_h, to_b):
+        pl.semaphore_signal(barrier, inc=1, device_id=(to_h, to_b), device_id_type=MESH)
+
+    each_other(greet)
 
     for g in range(nh * sub):
         cols = slice(g * gcols, (g + 1) * gcols)
@@ -102,23 +115,27 @@
     def local(src, dst, phase):
         pltpu.make_async_copy(src, dst, rsem.at[phase]).start()
 
-    def send_q(step, carry):
-        group = lax.rem(h * sub + k_own + step, nh * sub)
-        to_h, to_s = group // sub, lax.rem(group, sub)
-        remote(qs.at[group], qr.at[k_own * nh + h], 1, to_h, to_s * quarter + m_own)
-        return carry
-
-    lax.fori_loop(1, nh * sub, send_q, 0)
-    local(qs.at[h * sub + k_own], qr.at[k_own * nh + h], 1)
-
-    def send_kv(step, carry):
-        to = lax.rem(me + step, n)
-        to_h, to_b = to // nb, lax.rem(to, nb)
-        remote(kvs.at[to_h * sub + to_b // quarter], kvr.at[me], 0, to_h, to_b)
-        return carry
-
-    lax.fori_loop(1, n, send_kv, 0)
-    local(kvs.at[h * sub + k_own], kvr.at[me], 0)
+    for far in range(nh):
+        to_h = wrap(h + far, nh)
+        for step in range(sub):
+            to_s = wrap(k_own + step, sub)
+            source, target = qs.at[to_h * sub + to_s], qr.at[k_own * nh + h]
+            if far == 0 and step == 0:
+                local(source, target, 1)
+            else:
+                remote(source, target, 1, to_h, to_s * quarter + m_own)
+
+    for far in range(nh):
+        to_h = wrap(h + far, nh)
+
+        def send_kv(step, carry, to_h=to_h):
+            to_b = wrap(b + 2 * step, nb)
+            source = kvs.at[to_h * sub + lax.div(to_b, quarter)]
+            remote(source, kvr.at[side, half_me], 0, to_h, to_b)
+            return carry
+
+        lax.fori_loop(1 if far == 0 else 0, nb // 2, send_kv, 0, unroll=nb <= 16)
+    local(kvs.at[h * sub + k_own], kvr.at[side, half_me], 0)
 
     slots = nb * cap
     row = lax.broadcasted_iota(jnp.int32, (slots, tok), 0)
@@ -136,31 +153,45 @@
     pick = [jnp.where(choice & here, 1.0, 0.0) for choice in (first, second)]
     eye = lax.broadcasted_iota(jnp.int32, (tok, tok), 0) == lax.broadcasted_iota(jnp.int32, (tok, tok), 1)
 
+    wait_bytes(kvr.at[side], rsem.at[0])
+    pltpu.make_async_remote_copy(
+        src_ref=kvr.at[side], dst_ref=kvr.at[side], send_sem=ssem.at[6], recv_sem=rsem.at[6],
+        device_id=(h, b + 1 - 2 * side), device_id_type=MESH,
+    ).start()
     wait_bytes(qr, rsem.at[1])
-    wait_bytes(kvr, rsem.at[0])
 
     rows = nh * sub * tok
     queries = qr[...].reshape(rows, win)
-    keys = kvr[:, :, klo:kvcols].reshape(n * tok, win)
-    values = kvr[:, :, 0:win].reshape(n * tok, win)
     lane = lax.broadcasted_iota(jnp.int32, (rows, win), 1)
+    lows = [win - gcols + j * HD for j in range(heads)]
+    split_q = [
+        jnp.where((lane >= lo) & (lane < lo + HD), queries, jnp.zeros_like(queries)) for lo in lows
+    ]
+
+    def score_half(which):
+        keys = kvr[which, :, :, klo:kvcols].reshape(half * tok, win)
+        return [dot_nt(q_j, keys) * (1.0 / math.sqrt(HD)) for q_j in split_q]
+
+    near_scores = score_half(side)
+    near_values = kvr[side, :, :, 0:win].reshape(half * tok, win)
+    wait_bytes(kvr.at[1 - side], rsem.at[6])
+    far_scores = score_half(1 - side)
+    far_values = kvr[1 - side, :, :, 0:win].reshape(half * tok, win)
     attended = jnp.zeros((rows, win), F32)
     for j in range(heads):
-        lo = win - gcols + j * HD
-        q_j = jnp.where((lane >= lo) & (lane < lo + HD), queries, jnp.zeros_like(queries))
-        scores = dot_nt(q_j, keys) * (1.0 / math.sqrt(HD))
-        probs = jnp.exp(scores - jnp.max(scores, axis=1, keepdims=True))
-        total = jnp.sum(probs, axis=1, keepdims=True)
-        numer = dot(probs.astype(BF16), values)
+        peak = jnp.maximum(
+            jnp.max(near_scores[j], axis=1, keepdims=True), jnp.max(far_scores[j], axis=1, keepdims=True)
+        )
+        near = jnp.exp(near_scores[j] - peak)
+        far = jnp.exp(far_scores[j] - peak)
+        total = jnp.sum(near, axis=1, keepdims=True) + jnp.sum(far, axis=1, keepdims=True)
+        numer = dot(near.astype(BF16), near_values) + dot(far.astype(BF16), far_values)
         attended = jnp.where((lane >= j * HD) & (lane < (j + 1) * HD), numer / total, attended)
     ats[...] = attended.astype(BF16).reshape(sub, nh * tok, win)
 
-    def send_att(step, carry):
-        to_k = lax.rem(k_own + step, sub)
+    for step in range(1, sub):
+        to_k = wrap(k_own + step, sub)
         remote(ats.at[to_k], atr.at[k_own], 2, h, to_k * quarter + m_own)
-        return carry
-
-    lax.fori_loop(1, sub, send_att, 0)
     local(ats.at[k_own], atr.at[k_own], 2)
     fetch[0].wait()
     wait_bytes(atr, rsem.at[2])
@@ -170,12 +201,9 @@
         partial = partial + dot(atr[s, :, 0:gcols], ow[s * gcols:(s + 1) * gcols, :])
     ps[...] = partial.astype(BF16).reshape(nh, tok, width)
 
-    def send_part(step, carry):
-        to_h = lax.rem(h + step, nh)
+    for far in range(1, nh):
+        to_h = wrap(h + far, nh)
         remote(ps.at[to_h], pr.at[h], 3, to_h, b)
-        return carry
-
-    lax.fori_loop(1, nh, send_part, 0)
     local(ps.at[h], pr.at[h], 3)
     wait_bytes(pr, rsem.at[3])
 
@@ -194,13 +222,7 @@
         thin[pl.ds(c, slots, pieces), :] = buffer[:, c * LANES:(c + 1) * LANES]
     sb[...] = thin[...].reshape(sb.shape).astype(BF16)
 
-    def send_rows(step, carry):
-        to = lax.rem(me + step, n)
-        to_h, to_b = to // nb, lax.rem(to, nb)
-        remote(sb.at[to_b], xr.at[me], 4, to_h, to_b)
-        return carry
-
-    lax.fori_loop(1, n, send_rows, 0)
+    each_other(lambda to_h, to_b: remote(sb.at[to_b], xr.at[me], 4, to_h, to_b))
     local(sb.at[b], xr.at[me], 4)
     fetch[1].wait()
     wait_bytes(xr, rsem.at[4])
@@ -228,15 +250,11 @@
             wide[pl.ds(i * (down_tile // LANES) + c, n * cap, pieces), :] = part[:, c * LANES:(c + 1) * LANES]
     eb[...] = wide[...].reshape(eb.shape).astype(BF16)
 
-    def send_back(step, carry):
-        to = lax.rem(me + step, n)
-        remote(eb.at[to], rr.at[me], 5, to // nb, lax.rem(to, nb))
-        return carry
-
-    lax.fori_loop(1, n, send_back, 0)
+    each_other(lambda to_h, to_b: remote(eb.at[to_h * nb + to_b], rr.at[me], 5, to_h, to_b))
     local(eb.at[me], rr.at[me], 5)
 
-    wait_bytes(kvr.at[pl.ds(0, n - 1)], ssem.at[0])
+    wait_bytes(kvr.at[0, pl.ds(0, half - 1)], ssem.at[0])
+    wait_bytes(kvr.at[side], ssem.at[6])
     wait_bytes(qr.at[pl.ds(0, nh * sub - 1)], ssem.at[1])
     if sub > 1:
         wait_bytes(atr.at[pl.ds(0, sub - 1)], ssem.at[2])
@@ -277,7 +295,6 @@
     ff = expert_up.shape[2]
     vmem = pl.BlockSpec(memory_space=pltpu.VMEM)
     anywhere = pl.BlockSpec(memory_space=pl.ANY)
-    as_row = lambda vector: vector.reshape(1, width)
     return pl.pallas_call(
         functools.partial(kernel, (nh, nb, sub, cap)),
         out_shape=jax.ShapeDtypeStruct((tok, width), BF16),
@@ -288,7 +305,7 @@
             pltpu.VMEM(expert_up.shape[1:], BF16),
             pltpu.VMEM(expert_down.shape[1:], BF16),
             pltpu.VMEM((nh * sub, tok, kvcols), BF16),
-            pltpu.VMEM((n, tok, kvcols), BF16),
+            pltpu.VMEM((2, n // 2, tok, kvcols), BF16),
             pltpu.VMEM((nh * sub, tok, win), BF16),
             pltpu.VMEM((nh * sub, tok, win), BF16),
             pltpu.VMEM((sub, nh * tok, win), BF16),
@@ -305,8 +322,8 @@
             pltpu.VMEM((n * cap, ff), BF16),
             pltpu.VMEM((n * cap, width), BF16),
             pltpu.SemaphoreType.DMA((3,)),
-            pltpu.SemaphoreType.DMA((6,)),
-            pltpu.SemaphoreType.DMA((6,)),
+            pltpu.SemaphoreType.DMA((7,)),
+            pltpu.SemaphoreType.DMA((7,)),
         ],
         compiler_params=pltpu.CompilerParams(
             collective_id=0, has_side_effects=True, vmem_limit_bytes=60 * 1024 * 1024
@@ -314,7 +331,7 @@
         name="layer",
     )(
         query_rows, key_rows, value_rows, residual,
-        as_row(attention_gate), as_row(norm_shift), as_row(norm_scale), as_row(expert_gate),
+        attention_gate, norm_shift, norm_scale, expert_gate,
         routing.T, combine_weight.T,
         out_weight, expert_up, expert_down,
     )

time: 51.1 us -> 43.4 us (0.85)
  local copies, waits for them, and re-layouts: 6.59 us -> 1.42 us
  Pallas kernels: 44 us -> 41.7 us
    reshape x4 -> x0, local copies, waits for them, and re-layouts: 5.17 us -> none  [on_device(): as_row = lambda vector: vector.reshape(1, width)]
    pallas_call x1, Pallas kernels: 44 us -> 41.7 us  [on_device(): pl.pallas_call(functools.partial(kernel, (nh, nb, sub, cap)), out_shape=j...]
where the time goes in v2:
time: 43.4 us; the launch traced here: 43.2 us
  Pallas kernels  41.7 us (96%)
  local copies, waits for them, and re-layouts  1.42 us (3%)
    pallas_call x1, Pallas kernels, on_device(): pl.pallas_call(functools.partial(kernel, (nh, nb, sub, cap)), out_shape=j...  41.7 us
    unnamed x1, local copies, waits for them, and re-layouts  1.42 us

profile of v2, /device:TPU:0, one launch (start us, length us, event | category | flops | bytes accessed | tf_op | source)
XLA Modules:
  0.0 43.2 jit_solution(6697669307893529005)
XLA Ops:
  0.0 41.7 %layer.1 = bf16[16,1536]{1,0:T(8,128)(2,1)} custom-call(bf16[16,1536]{1,0:T(8,128)(2,1)} %q_ref.1, bf16[16,1536]{1,0:T(8,128)(2,1)} %k_ref.1, bf16[16,1536]{1,0:T(8,128)(2,1)} %v_ref.1, bf16[16,1536]{1,0:T(8,128)(2,1)} %res_ref.1, f32[1536]{0:T(1024)} %ag_ref.1, f32[1536]{0:T(1024)} %shift_ref.1, f32[1536]{0:T(1024)} %scale_ref.1, f32[1536]{0:T(1024)} %eg_ref.1, ...), custom_call_target="tpu_custom_call" | custom-call | tf_op jit(solution)/shard_map/layer/pallas_call | solution.py:298
  41.7 1.4 %copy.15 = bf16[16,1536]{1,0:T(8,128)(2,1)} copy(bf16[16,1536]{1,0:T(8,128)(2,1)} %layer.1) | data formatting | bytes 98304

commit v3 on v2

--- a/solution.py
+++ b/solution.py
@@ -42,13 +42,14 @@
 
 def kernel(
     dims,
-    q_ref, k_ref, v_ref, res_ref, ag_ref, shift_ref, scale_ref, eg_ref, route_ref, comb_ref,
+    q_hbm, k_hbm, v_hbm, res_hbm, ag_hbm, shift_hbm, scale_hbm, eg_hbm, route_hbm, comb_hbm,
     ow_hbm, up_hbm, down_hbm,
     out_ref,
+    q_ref, k_ref, v_ref, res_ref, ag_ref, shift_ref, scale_ref, eg_ref, route_ref, comb_ref,
     ow, up, down,
-    kvs, kvr, qs, qr, ats, atr, ps, pr, sb, xr, eb, rr,
+    kvs, kvr, qs, qr, ats, atr, ps, pr, sb, xr, es, er, eb, rr,
     mid, wide, thin, hidden, flat,
-    wsem, ssem, rsem,
+    isem, wsem, ssem, rsem, esend, erecv,
 ):
     nh, nb, sub, cap = dims
     n = nh * nb
@@ -69,6 +70,16 @@
     half = n // 2
     half_me = h * (nb // 2) + lax.div(b, 2)
 
+    inputs = [
+        pltpu.make_async_copy(source, target, isem.at[i])
+        for i, (source, target) in enumerate((
+            (v_hbm, v_ref), (k_hbm, k_ref), (q_hbm, q_ref), (res_hbm, res_ref), (ag_hbm, ag_ref),
+            (shift_hbm, shift_ref), (scale_hbm, scale_ref), (eg_hbm, eg_ref), (route_hbm, route_ref),
+            (comb_hbm, comb_ref),
+        ))
+    ]
+    for copy in inputs:
+        copy.start()
     fetch = [
         pltpu.make_async_copy(ow_hbm, ow, wsem.at[0]),
         pltpu.make_async_copy(up_hbm.at[0], up, wsem.at[1]),
@@ -93,6 +104,9 @@
         pl.semaphore_signal(barrier, inc=1, device_id=(to_h, to_b), device_id_type=MESH)
 
     each_other(greet)
+
+    for copy in inputs:
+        copy.wait()
 
     for g in range(nh * sub):
         cols = slice(g * gcols, (g + 1) * gcols)
@@ -164,29 +178,30 @@
     queries = qr[...].reshape(rows, win)
     lane = lax.broadcasted_iota(jnp.int32, (rows, win), 1)
     lows = [win - gcols + j * HD for j in range(heads)]
-    split_q = [
-        jnp.where((lane >= lo) & (lane < lo + HD), queries, jnp.zeros_like(queries)) for lo in lows
-    ]
+    split_q = jnp.concatenate(
+        [jnp.where((lane >= lo) & (lane < lo + HD), queries, jnp.zeros_like(queries)) for lo in lows], axis=0
+    )
 
     def score_half(which):
         keys = kvr[which, :, :, klo:kvcols].reshape(half * tok, win)
-        return [dot_nt(q_j, keys) * (1.0 / math.sqrt(HD)) for q_j in split_q]
+        return dot_nt(split_q, keys) * (1.0 / math.sqrt(HD))
 
     near_scores = score_half(side)
+    near_peak = jnp.max(near_scores, axis=1, keepdims=True)
     near_values = kvr[side, :, :, 0:win].reshape(half * tok, win)
     wait_bytes(kvr.at[1 - side], rsem.at[6])
     far_scores = score_half(1 - side)
     far_values = kvr[1 - side, :, :, 0:win].reshape(half * tok, win)
+    peak = jnp.maximum(near_peak, jnp.max(far_scores, axis=1, keepdims=True))
+    near = jnp.exp(near_scores - peak)
+    far = jnp.exp(far_scores - peak)
+    total = jnp.sum(near, axis=1, keepdims=True) + jnp.sum(far, axis=1, keepdims=True)
+    stacked = (dot(near.astype(BF16), near_values) + dot(far.astype(BF16), far_values)) / total
     attended = jnp.zeros((rows, win), F32)
     for j in range(heads):
-        peak = jnp.maximum(
-            jnp.max(near_scores[j], axis=1, keepdims=True), jnp.max(far_scores[j], axis=1, keepdims=True)
+        attended = jnp.where(
+            (lane >= j * HD) & (lane < (j + 1) * HD), stacked[j * rows:(j + 1) * rows], attended
         )
-        near = jnp.exp(near_scores[j] - peak)
-        far = jnp.exp(far_scores[j] - peak)
-        total = jnp.sum(near, axis=1, keepdims=True) + jnp.sum(far, axis=1, keepdims=True)
-        numer = dot(near.astype(BF16), near_values) + dot(far.astype(BF16), far_values)
-        attended = jnp.where((lane >= j * HD) & (lane < (j + 1) * HD), numer / total, attended)
     ats[...] = attended.astype(BF16).reshape(sub, nh * tok, win)
 
     for step in range(1, sub):
@@ -243,15 +258,37 @@
 
     lax.fori_loop(0, ff // up_tile, up_step, 0)
     fetch[2].wait()
-    down_tile = math.gcd(width, 512)
-    for i in range(width // down_tile):
+    tiles, _, back_rows, down_tile = es.shape
+    tile_pieces = down_tile // LANES
+
+    def tile_copy(i, far):
+        to_h = wrap(h + far, nh)
+        return pltpu.make_async_remote_copy(
+            src_ref=es.at[i, to_h], dst_ref=er.at[i, far - 1], send_sem=esend.at[i, far - 1],
+            recv_sem=erecv.at[i, far - 1], device_id=(to_h, b), device_id_type=MESH,
+        )
+
+    for i in range(tiles):
         part = dot(hidden[...], down[:, i * down_tile:(i + 1) * down_tile])
-        for c in range(down_tile // LANES):
-            wide[pl.ds(i * (down_tile // LANES) + c, n * cap, pieces), :] = part[:, c * LANES:(c + 1) * LANES]
-    eb[...] = wide[...].reshape(eb.shape).astype(BF16)
-
-    each_other(lambda to_h, to_b: remote(eb.at[to_h * nb + to_b], rr.at[me], 5, to_h, to_b))
-    local(eb.at[me], rr.at[me], 5)
+        es[i] = part.astype(BF16).reshape(nh, back_rows, down_tile)
+        for far in range(1, nh):
+            tile_copy(i, far).start()
+    for i in range(tiles):
+        both = es[i, h].astype(F32)
+        for far in range(1, nh):
+            tile_copy(i, far).wait_recv()
+            both = both + er[i, far - 1].astype(F32)
+        for c in range(tile_pieces):
+            thin[pl.ds(i * tile_pieces + c, slots, pieces), :] = both[:, c * LANES:(c + 1) * LANES]
+    eb[...] = thin[...].reshape(eb.shape).astype(BF16)
+
+    def send_back(step, carry):
+        to_b = wrap(b + step, nb)
+        remote(eb.at[to_b], rr.at[b], 5, h, to_b)
+        return carry
+
+    lax.fori_loop(1, nb, send_back, 0, unroll=nb <= 16)
+    local(eb.at[b], rr.at[b], 5)
 
     wait_bytes(kvr.at[0, pl.ds(0, half - 1)], ssem.at[0])
     wait_bytes(kvr.at[side], ssem.at[6])
@@ -262,10 +299,7 @@
     wait_bytes(xr.at[pl.ds(0, n - 1)], ssem.at[4])
 
     wait_bytes(rr, rsem.at[5])
-    summed = rr[0:nb].astype(F32)
-    for other in range(1, nh):
-        summed = summed + rr[other * nb:(other + 1) * nb].astype(F32)
-    thin[...] = summed.reshape(thin.shape)
+    thin[...] = rr[...].astype(F32).reshape(thin.shape)
     weights = [
         jnp.sum(jnp.where(eye, comb_ref[i:i + 1, :], 0.0), axis=1, keepdims=True) for i in range(TOPK)
     ]
@@ -275,7 +309,10 @@
     mixture = weights[0] * dot_tn(pick[0].astype(BF16), back)
     mixture = mixture + weights[1] * dot_tn(pick[1].astype(BF16), back)
     out_ref[...] = (mid[...] + eg_ref[...] * mixture).astype(BF16)
-    wait_bytes(rr.at[pl.ds(0, n - 1)], ssem.at[5])
+    wait_bytes(rr.at[pl.ds(0, nb - 1)], ssem.at[5])
+    for i in range(tiles):
+        for far in range(1, nh):
+            tile_copy(i, far).wait_send()
 
 
 def on_device(
@@ -293,14 +330,21 @@
     pieces = width // LANES
     block = cap * pieces
     ff = expert_up.shape[2]
+    down_tile = math.gcd(width, 512)
+    tiles = width // down_tile
+    small = (
+        query_rows, key_rows, value_rows, residual, attention_gate, norm_shift, norm_scale, expert_gate,
+        routing.T, combine_weight.T,
+    )
     vmem = pl.BlockSpec(memory_space=pltpu.VMEM)
     anywhere = pl.BlockSpec(memory_space=pl.ANY)
     return pl.pallas_call(
         functools.partial(kernel, (nh, nb, sub, cap)),
         out_shape=jax.ShapeDtypeStruct((tok, width), BF16),
-        in_specs=[vmem] * 10 + [anywhere] * 3,
+        in_specs=[anywhere] * 13,
         out_specs=vmem,
         scratch_shapes=[
+            *[pltpu.VMEM(array.shape, array.dtype) for array in small],
             pltpu.VMEM(out_weight.shape, BF16),
             pltpu.VMEM(expert_up.shape[1:], BF16),
             pltpu.VMEM(expert_down.shape[1:], BF16),
@@ -314,27 +358,27 @@
             pltpu.VMEM((nh, tok, width), BF16),
             pltpu.VMEM((nb, block, LANES), BF16),
             pltpu.VMEM((n, block, LANES), BF16),
-            pltpu.VMEM((n, block, LANES), BF16),
-            pltpu.VMEM((n, block, LANES), BF16),
+            pltpu.VMEM((tiles, nh, nb * cap, down_tile), BF16),
+            pltpu.VMEM((tiles, nh - 1, nb * cap, down_tile), BF16),
+            pltpu.VMEM((nb, block, LANES), BF16),
+            pltpu.VMEM((nb, block, LANES), BF16),
             pltpu.VMEM((tok, width), F32),
             pltpu.VMEM((n * block, LANES), F32),
             pltpu.VMEM((nb * block, LANES), F32),
             pltpu.VMEM((n * cap, ff), BF16),
             pltpu.VMEM((n * cap, width), BF16),
+            pltpu.SemaphoreType.DMA((len(small),)),
             pltpu.SemaphoreType.DMA((3,)),
             pltpu.SemaphoreType.DMA((7,)),
             pltpu.SemaphoreType.DMA((7,)),
+            pltpu.SemaphoreType.DMA((tiles, nh - 1)),
+            pltpu.SemaphoreType.DMA((tiles, nh - 1)),
         ],
         compiler_params=pltpu.CompilerParams(
             collective_id=0, has_side_effects=True, vmem_limit_bytes=60 * 1024 * 1024
         ),
         name="layer",
-    )(
-        query_rows, key_rows, value_rows, residual,
-        attention_gate, norm_shift, norm_scale, expert_gate,
-        routing.T, combine_weight.T,
-        out_weight, expert_up, expert_down,
-    )
+    )(*small, out_weight, expert_up, expert_down)
 
 
 def solution(mesh):

time: 43.4 us -> 44.3 us (1.021)
  Pallas kernels: 41.7 us -> 42.7 us
    pallas_call x1, Pallas kernels: 41.7 us -> 42.7 us  [on_device(): pl.pallas_call(functools.partial(kernel, (nh, nb, sub, cap)), out_shape=j...]
where the time goes in v3:
time: 44.3 us; the launch traced here: 44.1 us
  Pallas kernels  42.7 us (96%)
  local copies, waits for them, and re-layouts  1.42 us (3%)
    pallas_call x1, Pallas kernels, on_device(): pl.pallas_call(functools.partial(kernel, (nh, nb, sub, cap)), out_shape=j...  42.7 us
    unnamed x1, local copies, waits for them, and re-layouts  1.42 us

profile of v3, /device:TPU:0, one launch (start us, length us, event | category | flops | bytes accessed | tf_op | source)
XLA Modules:
  0.0 44.1 jit_solution(10199253103814444882)
XLA Ops:
  0.0 42.7 %layer.1 = bf16[16,1536]{1,0:T(8,128)(2,1)} custom-call(bf16[16,1536]{1,0:T(8,128)(2,1)} %q_hbm.1, bf16[16,1536]{1,0:T(8,128)(2,1)} %k_hbm.1, bf16[16,1536]{1,0:T(8,128)(2,1)} %v_hbm.1, bf16[16,1536]{1,0:T(8,128)(2,1)} %res_hbm.1, f32[1536]{0:T(1024)} %ag_hbm.1, f32[1536]{0:T(1024)} %shift_hbm.1, f32[1536]{0:T(1024)} %scale_hbm.1, f32[1536]{0:T(1024)} %eg_hbm.1, ...), custom_call_target="tpu_custom_call" | custom-call | tf_op jit(solution)/shard_map/layer/pallas_call | solution.py:341
  42.7 1.4 %copy.15 = bf16[16,1536]{1,0:T(8,128)(2,1)} copy(bf16[16,1536]{1,0:T(8,128)(2,1)} %layer.1) | data formatting | bytes 98304

commit v4 on v3

--- a/solution.py
+++ b/solution.py
@@ -47,10 +47,13 @@
     out_ref,
     q_ref, k_ref, v_ref, res_ref, ag_ref, shift_ref, scale_ref, eg_ref, route_ref, comb_ref,
     ow, up, down,
-    kvs, kvr, qs, qr, ats, atr, ps, pr, sb, xr, es, er, eb, rr,
-    mid, wide, thin, hidden, flat,
-    isem, wsem, ssem, rsem, esend, erecv,
+    kvs, kvr, qs, qr, ats, atr, ps, pr,
+    mid, wide, thin, hidden, held,
+    isem, wsem, ssem, rsem, csem,
+    *chunked,
 ):
+    sb, xr, eb, rr, flat = (chunked[i::5] for i in range(5))
+    chunks = len(sb)
     nh, nb, sub, cap = dims
     n = nh * nb
     quarter = nb // sub
@@ -91,14 +94,15 @@
     barrier = pltpu.get_barrier_semaphore()
 
     def each_other(act):
-        for far in range(nh):
+        paired = nb & (nb - 1) == 0
+        for far in reversed(range(nh)):
             to_h = wrap(h + far, nh)
 
             def step_to(step, carry, to_h=to_h):
-                act(to_h, wrap(b + step, nb))
+                act(to_h, lax.bitwise_xor(b, nb - 1 - step) if paired else wrap(b + nb - 1 - step, nb))
                 return carry
 
-            lax.fori_loop(1 if far == 0 else 0, nb, step_to, 0, unroll=nb <= 16)
+            lax.fori_loop(0, nb - 1 if far == 0 else nb, step_to, 0, unroll=nb <= 16)
 
     def greet(to_h, to_b):
         pl.semaphore_signal(barrier, inc=1, device_id=(to_h, to_b), device_id_type=MESH)
@@ -120,11 +124,17 @@
 
     pl.semaphore_wait(barrier, n - 1)
 
-    def remote(src, dst, phase, to_h, to_b):
+    def remote(src, dst, phase, to_h, to_b, sends=ssem, receives=rsem):
         pltpu.make_async_remote_copy(
-            src_ref=src, dst_ref=dst, send_sem=ssem.at[phase], recv_sem=rsem.at[phase],
+            src_ref=src, dst_ref=dst, send_sem=sends.at[phase], recv_sem=receives.at[phase],
             device_id=(to_h, to_b), device_id_type=MESH,
         ).start()
+
+    def scatter(source_of, target, row):
+        each_other(
+            lambda to_h, to_b: remote(source_of(to_h, to_b), target.at[me], row, to_h, to_b, csem.at[0], csem.at[1])
+        )
+        pltpu.make_async_copy(source_of(h, b), target.at[me], csem.at[1, row]).start()
 
     def local(src, dst, phase):
         pltpu.make_async_copy(src, dst, rsem.at[phase]).start()
@@ -232,63 +242,50 @@
     ).astype(BF16)
     mid[...] = middle
 
+    spans = []
+    for ref in sb:
+        start = spans[-1][1] if spans else 0
+        spans.append((start, start + ref.shape[1] // cap * LANES))
     buffer = dot((pick[0] + pick[1]).astype(BF16), normed)
-    for c in range(pieces):
-        thin[pl.ds(c, slots, pieces), :] = buffer[:, c * LANES:(c + 1) * LANES]
-    sb[...] = thin[...].reshape(sb.shape).astype(BF16)
-
-    each_other(lambda to_h, to_b: remote(sb.at[to_b], xr.at[me], 4, to_h, to_b))
-    local(sb.at[b], xr.at[me], 4)
-    fetch[1].wait()
-    wait_bytes(xr, rsem.at[4])
-
-    wide[...] = xr[...].astype(F32).reshape(wide.shape)
-    for c in range(pieces):
-        flat[:, c * LANES:(c + 1) * LANES] = wide[pl.ds(c, n * cap, pieces), :].astype(BF16)
+    for i, (start, stop) in enumerate(spans):
+        count = (stop - start) // LANES
+        for c in range(count):
+            thin[pl.ds(c, slots, count), :] = buffer[:, start + c * LANES:start + (c + 1) * LANES]
+        sb[i][...] = thin[0:slots * count].reshape(sb[i].shape).astype(BF16)
+        scatter(lambda to_h, to_b: sb[i].at[to_b], xr[i], i)
 
     ff = up.shape[1]
     up_tile = math.gcd(ff, 512)
-
-    def up_step(i, carry):
-        cols = pl.ds(pl.multiple_of(i * up_tile, up_tile), up_tile)
-        u = dot(flat[...], up[:, cols])
-        inner = math.sqrt(2.0 / math.pi) * (u + 0.044715 * (u * u * u))
-        hidden[:, cols] = (0.5 * u * (1.0 + jnp.tanh(inner))).astype(BF16)
-        return carry
-
-    lax.fori_loop(0, ff // up_tile, up_step, 0)
+    fetch[1].wait()
+    for i, (start, stop) in enumerate(spans):
+        count = (stop - start) // LANES
+        wait_bytes(xr[i], csem.at[1, i])
+        wide[0:n * cap * count] = xr[i][...].astype(F32).reshape(n * cap * count, LANES)
+        for c in range(count):
+            flat[i][:, c * LANES:(c + 1) * LANES] = wide[pl.ds(c, n * cap, count), :].astype(BF16)
+
+        def up_step(t, carry, i=i, start=start, stop=stop):
+            cols = pl.ds(pl.multiple_of(t * up_tile, up_tile), up_tile)
+            u = dot(flat[i][...], up[start:stop, cols])
+            if i > 0:
+                u = held[:, cols] + u
+            if i < chunks - 1:
+                held[:, cols] = u
+            else:
+                inner = math.sqrt(2.0 / math.pi) * (u + 0.044715 * (u * u * u))
+                hidden[:, cols] = (0.5 * u * (1.0 + jnp.tanh(inner))).astype(BF16)
+            return carry
+
+        lax.fori_loop(0, ff // up_tile, up_step, 0)
+
     fetch[2].wait()
-    tiles, _, back_rows, down_tile = es.shape
-    tile_pieces = down_tile // LANES
-
-    def tile_copy(i, far):
-        to_h = wrap(h + far, nh)
-        return pltpu.make_async_remote_copy(
-            src_ref=es.at[i, to_h], dst_ref=er.at[i, far - 1], send_sem=esend.at[i, far - 1],
-            recv_sem=erecv.at[i, far - 1], device_id=(to_h, b), device_id_type=MESH,
-        )
-
-    for i in range(tiles):
-        part = dot(hidden[...], down[:, i * down_tile:(i + 1) * down_tile])
-        es[i] = part.astype(BF16).reshape(nh, back_rows, down_tile)
-        for far in range(1, nh):
-            tile_copy(i, far).start()
-    for i in range(tiles):
-        both = es[i, h].astype(F32)
-        for far in range(1, nh):
-            tile_copy(i, far).wait_recv()
-            both = both + er[i, far - 1].astype(F32)
-        for c in range(tile_pieces):
-            thin[pl.ds(i * tile_pieces + c, slots, pieces), :] = both[:, c * LANES:(c + 1) * LANES]
-    eb[...] = thin[...].reshape(eb.shape).astype(BF16)
-
-    def send_back(step, carry):
-        to_b = wrap(b + step, nb)
-        remote(eb.at[to_b], rr.at[b], 5, h, to_b)
-        return carry
-
-    lax.fori_loop(1, nb, send_back, 0, unroll=nb <= 16)
-    local(eb.at[b], rr.at[b], 5)
+    for i, (start, stop) in enumerate(spans):
+        count = (stop - start) // LANES
+        part = dot(hidden[...], down[:, start:stop])
+        for c in range(count):
+            wide[pl.ds(c, n * cap, count), :] = part[:, c * LANES:(c + 1) * LANES]
+        eb[i][...] = wide[0:n * cap * count].reshape(eb[i].shape).astype(BF16)
+        scatter(lambda to_h, to_b: eb[i].at[to_h * nb + to_b], rr[i], chunks + i)
 
     wait_bytes(kvr.at[0, pl.ds(0, half - 1)], ssem.at[0])
     wait_bytes(kvr.at[side], ssem.at[6])
@@ -296,23 +293,25 @@
     if sub > 1:
         wait_bytes(atr.at[pl.ds(0, sub - 1)], ssem.at[2])
     wait_bytes(pr.at[pl.ds(0, nh - 1)], ssem.at[3])
-    wait_bytes(xr.at[pl.ds(0, n - 1)], ssem.at[4])
-
-    wait_bytes(rr, rsem.at[5])
-    thin[...] = rr[...].astype(F32).reshape(thin.shape)
     weights = [
         jnp.sum(jnp.where(eye, comb_ref[i:i + 1, :], 0.0), axis=1, keepdims=True) for i in range(TOPK)
     ]
-    back = jnp.concatenate(
-        [thin[pl.ds(c, slots, pieces), :].astype(BF16) for c in range(pieces)], axis=1
-    )
-    mixture = weights[0] * dot_tn(pick[0].astype(BF16), back)
-    mixture = mixture + weights[1] * dot_tn(pick[1].astype(BF16), back)
-    out_ref[...] = (mid[...] + eg_ref[...] * mixture).astype(BF16)
-    wait_bytes(rr.at[pl.ds(0, nb - 1)], ssem.at[5])
-    for i in range(tiles):
-        for far in range(1, nh):
-            tile_copy(i, far).wait_send()
+    for i, (start, stop) in enumerate(spans):
+        count = (stop - start) // LANES
+        wait_bytes(xr[i].at[pl.ds(0, n - 1)], csem.at[0, i])
+        wait_bytes(rr[i], csem.at[1, chunks + i])
+        summed = rr[i][0:nb].astype(F32)
+        for other in range(1, nh):
+            summed = summed + rr[i][other * nb:(other + 1) * nb].astype(F32)
+        thin[0:slots * count] = summed.reshape(slots * count, LANES)
+        back = jnp.concatenate(
+            [thin[pl.ds(c, slots, count), :].astype(BF16) for c in range(count)], axis=1
+        )
+        mixture = weights[0] * dot_tn(pick[0].astype(BF16), back)
+        mixture = mixture + weights[1] * dot_tn(pick[1].astype(BF16), back)
+        out_ref[:, start:stop] = mid[:, start:stop] + eg_ref[start:stop] * mixture
+    for i in range(chunks):
+        wait_bytes(rr[i].at[pl.ds(0, n - 1)], csem.at[0, chunks + i])
 
 
 def on_device(
@@ -328,10 +327,10 @@
     win = round_up(gcols, LANES)
     kvcols = round_up(2 * gcols, LANES)
     pieces = width // LANES
-    block = cap * pieces
+    last = max(1, pieces // 12) * 4 if pieces % 4 == 0 and pieces > 4 else 0
+    counts = [count for count in (pieces - last, last) if count]
+    most = max(counts) * cap
     ff = expert_up.shape[2]
-    down_tile = math.gcd(width, 512)
-    tiles = width // down_tile
     small = (
         query_rows, key_rows, value_rows, residual, attention_gate, norm_shift, norm_scale, expert_gate,
         routing.T, combine_weight.T,
@@ -340,7 +339,7 @@
     anywhere = pl.BlockSpec(memory_space=pl.ANY)
     return pl.pallas_call(
         functools.partial(kernel, (nh, nb, sub, cap)),
-        out_shape=jax.ShapeDtypeStruct((tok, width), BF16),
+        out_shape=jax.ShapeDtypeStruct((tok, width), F32),
         in_specs=[anywhere] * 13,
         out_specs=vmem,
         scratch_shapes=[
@@ -356,29 +355,33 @@
             pltpu.VMEM((sub, nh * tok, win), BF16),
             pltpu.VMEM((nh, tok, width), BF16),
             pltpu.VMEM((nh, tok, width), BF16),
-            pltpu.VMEM((nb, block, LANES), BF16),
-            pltpu.VMEM((n, block, LANES), BF16),
-            pltpu.VMEM((tiles, nh, nb * cap, down_tile), BF16),
-            pltpu.VMEM((tiles, nh - 1, nb * cap, down_tile), BF16),
-            pltpu.VMEM((nb, block, LANES), BF16),
-            pltpu.VMEM((nb, block, LANES), BF16),
             pltpu.VMEM((tok, width), F32),
-            pltpu.VMEM((n * block, LANES), F32),
-            pltpu.VMEM((nb * block, LANES), F32),
+            pltpu.VMEM((n * most, LANES), F32),
+            pltpu.VMEM((nb * most, LANES), F32),
             pltpu.VMEM((n * cap, ff), BF16),
-            pltpu.VMEM((n * cap, width), BF16),
+            pltpu.VMEM((n * cap, ff), F32),
             pltpu.SemaphoreType.DMA((len(small),)),
             pltpu.SemaphoreType.DMA((3,)),
             pltpu.SemaphoreType.DMA((7,)),
             pltpu.SemaphoreType.DMA((7,)),
-            pltpu.SemaphoreType.DMA((tiles, nh - 1)),
-            pltpu.SemaphoreType.DMA((tiles, nh - 1)),
+            pltpu.SemaphoreType.DMA((2, 2 * len(counts))),
+            *[
+                shape
+                for count in counts
+                for shape in (
+                    pltpu.VMEM((nb, cap * count, LANES), BF16),
+                    pltpu.VMEM((n, cap * count, LANES), BF16),
+                    pltpu.VMEM((n, cap * count, LANES), BF16),
+                    pltpu.VMEM((n, cap * count, LANES), BF16),
+                    pltpu.VMEM((n * cap, count * LANES), BF16),
+                )
+            ],
         ],
         compiler_params=pltpu.CompilerParams(
             collective_id=0, has_side_effects=True, vmem_limit_bytes=60 * 1024 * 1024
         ),
         name="layer",
-    )(*small, out_weight, expert_up, expert_down)
+    )(*small, out_weight, expert_up, expert_down).astype(BF16)
 
 
 def solution(mesh):

time: 44.3 us -> 42.2 us (0.953)
  Pallas kernels: 42.7 us -> 40.5 us
  other arithmetic: 0 us -> 1.52 us
  local copies, waits for them, and re-layouts: 1.42 us -> 0 us
    pallas_call x1, Pallas kernels: 42.7 us -> 40.5 us  [on_device(): pl.pallas_call(functools.partial(kernel, (nh, nb, sub, cap)), out_shape=j...]
    convert_element_type x0 -> x1, other arithmetic: none -> 1.52 us  [on_device(): return pl.pallas_call(functools.partial(kernel, (nh, nb, sub, cap)), out_...]
    unnamed x1 -> x0, local copies, waits for them, and re-layouts: 1.42 us -> none
where the time goes in v4:
time: 42.2 us; the launch traced here: 42.1 us
  Pallas kernels  40.5 us (96%)
  other arithmetic  1.52 us (4%)
    pallas_call x1, Pallas kernels, on_device(): pl.pallas_call(functools.partial(kernel, (nh, nb, sub, cap)), out_shape=j...  40.5 us
    convert_element_type x1, other arithmetic, on_device(): return pl.pallas_call(functools.partial(kernel, (nh, nb, sub, cap)), out_...  1.52 us

profile of v4, /device:TPU:0, one launch (start us, length us, event | category | flops | bytes accessed | tf_op | source)
XLA Modules:
  0.0 42.1 jit_solution(7781413169862678597)
XLA Ops:
  0.0 40.5 %layer.1 = f32[16,1536]{1,0:T(8,128)} custom-call(bf16[16,1536]{1,0:T(8,128)(2,1)} %q_hbm.1, bf16[16,1536]{1,0:T(8,128)(2,1)} %k_hbm.1, bf16[16,1536]{1,0:T(8,128)(2,1)} %v_hbm.1, bf16[16,1536]{1,0:T(8,128)(2,1)} %res_hbm.1, f32[1536]{0:T(1024)} %ag_hbm.1, f32[1536]{0:T(1024)} %shift_hbm.1, f32[1536]{0:T(1024)} %scale_hbm.1, f32[1536]{0:T(1024)} %eg_hbm.1, ...), custom_call_target="tpu_custom_call" | custom-call | tf_op jit(solution)/shard_map/layer/pallas_call | solution.py:340
  40.5 1.5 %convert_element_type.3 = bf16[16,1536]{1,0:T(8,128)(2,1)} convert(f32[16,1536]{1,0:T(8,128)} %layer.1) | non-fusion elementwise | flops 24576 | bytes 147456 | tf_op jit(solution)/shard_map/convert_element_type | solution.py:384

commit v5 on v4

--- a/solution.py
+++ b/solution.py
@@ -49,7 +49,7 @@
     ow, up, down,
     kvs, kvr, qs, qr, ats, atr, ps, pr,
     mid, wide, thin, hidden, held,
-    isem, wsem, ssem, rsem, csem,
+    isem, wsem, ssem, rsem, csem, psem,
     *chunked,
 ):
     sb, xr, eb, rr, flat = (chunked[i::5] for i in range(5))
@@ -73,6 +73,24 @@
     half = n // 2
     half_me = h * (nb // 2) + lax.div(b, 2)
 
+    barrier = pltpu.get_barrier_semaphore()
+
+    def each_other(act):
+        paired = nb & (nb - 1) == 0
+        for far in reversed(range(nh)):
+            to_h = wrap(h + far, nh)
+
+            def step_to(step, carry, to_h=to_h):
+                act(to_h, lax.bitwise_xor(b, nb - 1 - step) if paired else wrap(b + nb - 1 - step, nb))
+                return carry
+
+            lax.fori_loop(0, nb - 1 if far == 0 else nb, step_to, 0, unroll=nb <= 16)
+
+    def greet(to_h, to_b):
+        pl.semaphore_signal(barrier, inc=1, device_id=(to_h, to_b), device_id_type=MESH)
+
+    each_other(greet)
+
     inputs = [
         pltpu.make_async_copy(source, target, isem.at[i])
         for i, (source, target) in enumerate((
@@ -91,36 +109,14 @@
     for copy in fetch:
         copy.start()
 
-    barrier = pltpu.get_barrier_semaphore()
-
-    def each_other(act):
-        paired = nb & (nb - 1) == 0
-        for far in reversed(range(nh)):
-            to_h = wrap(h + far, nh)
-
-            def step_to(step, carry, to_h=to_h):
-                act(to_h, lax.bitwise_xor(b, nb - 1 - step) if paired else wrap(b + nb - 1 - step, nb))
-                return carry
-
-            lax.fori_loop(0, nb - 1 if far == 0 else nb, step_to, 0, unroll=nb <= 16)
-
-    def greet(to_h, to_b):
-        pl.semaphore_signal(barrier, inc=1, device_id=(to_h, to_b), device_id_type=MESH)
-
-    each_other(greet)
-
-    for copy in inputs:
+    for copy in inputs[:2]:
         copy.wait()
-
     for g in range(nh * sub):
         cols = slice(g * gcols, (g + 1) * gcols)
         kvs[g, :, 0:gcols] = v_ref[:, cols]
         kvs[g, :, kvcols - gcols:kvcols] = k_ref[:, cols]
         if kvcols > 2 * gcols:
             kvs[g, :, gcols:kvcols - gcols] = jnp.zeros((tok, kvcols - 2 * gcols), BF16)
-        if win > gcols:
-            qs[g, :, 0:win - gcols] = jnp.zeros((tok, win - gcols), BF16)
-        qs[g, :, win - gcols:win] = q_ref[:, cols]
 
     pl.semaphore_wait(barrier, n - 1)
 
@@ -139,6 +135,24 @@
     def local(src, dst, phase):
         pltpu.make_async_copy(src, dst, rsem.at[phase]).start()
 
+    for far in range(nh):
+        to_h = wrap(h + far, nh)
+
+        def send_kv(step, carry, to_h=to_h):
+            to_b = wrap(b + 2 * step, nb)
+            source = kvs.at[to_h * sub + lax.div(to_b, quarter)]
+            remote(source, kvr.at[side, half_me], 0, to_h, to_b)
+            return carry
+
+        lax.fori_loop(1 if far == 0 else 0, nb // 2, send_kv, 0, unroll=nb <= 16)
+    local(kvs.at[h * sub + k_own], kvr.at[side, half_me], 0)
+
+    inputs[2].wait()
+    for g in range(nh * sub):
+        cols = slice(g * gcols, (g + 1) * gcols)
+        if win > gcols:
+            qs[g, :, 0:win - gcols] = jnp.zeros((tok, win - gcols), BF16)
+        qs[g, :, win - gcols:win] = q_ref[:, cols]
     for far in range(nh):
         to_h = wrap(h + far, nh)
         for step in range(sub):
@@ -149,17 +163,8 @@
             else:
                 remote(source, target, 1, to_h, to_s * quarter + m_own)
 
-    for far in range(nh):
-        to_h = wrap(h + far, nh)
-
-        def send_kv(step, carry, to_h=to_h):
-            to_b = wrap(b + 2 * step, nb)
-            source = kvs.at[to_h * sub + lax.div(to_b, quarter)]
-            remote(source, kvr.at[side, half_me], 0, to_h, to_b)
-            return carry
-
-        lax.fori_loop(1 if far == 0 else 0, nb // 2, send_kv, 0, unroll=nb <= 16)
-    local(kvs.at[h * sub + k_own], kvr.at[side, half_me], 0)
+    for copy in inputs[3:]:
+        copy.wait()
 
     slots = nb * cap
     row = lax.broadcasted_iota(jnp.int32, (slots, tok), 0)
@@ -221,18 +226,32 @@
     fetch[0].wait()
     wait_bytes(atr, rsem.at[2])
 
-    partial = jnp.zeros((nh * tok, width), F32)
-    for s in range(sub):
-        partial = partial + dot(atr[s, :, 0:gcols], ow[s * gcols:(s + 1) * gcols, :])
-    ps[...] = partial.astype(BF16).reshape(nh, tok, width)
-
-    for far in range(1, nh):
+    splits, _, _, part_tile = ps.shape
+
+    def part_copy(i, far):
         to_h = wrap(h + far, nh)
-        remote(ps.at[to_h], pr.at[h], 3, to_h, b)
-    local(ps.at[h], pr.at[h], 3)
-    wait_bytes(pr, rsem.at[3])
-
-    projected = jnp.sum(pr[...].astype(F32), axis=0)
+        return pltpu.make_async_remote_copy(
+            src_ref=ps.at[i, to_h], dst_ref=pr.at[i, far - 1], send_sem=psem.at[0, i, far - 1],
+            recv_sem=psem.at[1, i, far - 1], device_id=(to_h, b), device_id_type=MESH,
+        )
+
+    for i in range(splits):
+        partial = jnp.zeros((nh * tok, part_tile), F32)
+        for s in range(sub):
+            partial = partial + dot(
+                atr[s, :, 0:gcols], ow[s * gcols:(s + 1) * gcols, i * part_tile:(i + 1) * part_tile]
+            )
+        ps[i] = partial.astype(BF16).reshape(nh, tok, part_tile)
+        for far in range(1, nh):
+            part_copy(i, far).start()
+    sums = []
+    for i in range(splits):
+        both = ps[i, h].astype(F32)
+        for far in range(1, nh):
+            part_copy(i, far).wait_recv()
+            both = both + pr[i, far - 1].astype(F32)
+        sums.append(both)
+    projected = jnp.concatenate(sums, axis=1)
     middle = res_ref[...].astype(F32) + ag_ref[...] * projected
     average = jnp.mean(middle, axis=1, keepdims=True)
     centered = middle - average
@@ -292,7 +311,9 @@
     wait_bytes(qr.at[pl.ds(0, nh * sub - 1)], ssem.at[1])
     if sub > 1:
         wait_bytes(atr.at[pl.ds(0, sub - 1)], ssem.at[2])
-    wait_bytes(pr.at[pl.ds(0, nh - 1)], ssem.at[3])
+    for i in range(splits):
+        for far in range(1, nh):
+            part_copy(i, far).wait_send()
     weights = [
         jnp.sum(jnp.where(eye, comb_ref[i:i + 1, :], 0.0), axis=1, keepdims=True) for i in range(TOPK)
     ]
@@ -327,6 +348,8 @@
     win = round_up(gcols, LANES)
     kvcols = round_up(2 * gcols, LANES)
     pieces = width // LANES
+    part_tile = math.gcd(width, 768)
+    splits = width // part_tile
     last = max(1, pieces // 12) * 4 if pieces % 4 == 0 and pieces > 4 else 0
     counts = [count for count in (pieces - last, last) if count]
     most = max(counts) * cap
@@ -339,7 +362,7 @@
     anywhere = pl.BlockSpec(memory_space=pl.ANY)
     return pl.pallas_call(
         functools.partial(kernel, (nh, nb, sub, cap)),
-        out_shape=jax.ShapeDtypeStruct((tok, width), F32),
+        out_shape=pltpu.VMEM((tok, width), F32),
         in_specs=[anywhere] * 13,
         out_specs=vmem,
         scratch_shapes=[
@@ -353,8 +376,8 @@
             pltpu.VMEM((nh * sub, tok, win), BF16),
             pltpu.VMEM((sub, nh * tok, win), BF16),
             pltpu.VMEM((sub, nh * tok, win), BF16),
-            pltpu.VMEM((nh, tok, width), BF16),
-            pltpu.VMEM((nh, tok, width), BF16),
+            pltpu.VMEM((splits, nh, tok, part_tile), BF16),
+            pltpu.VMEM((splits, nh - 1, tok, part_tile), BF16),
             pltpu.VMEM((tok, width), F32),
             pltpu.VMEM((n * most, LANES), F32),
             pltpu.VMEM((nb * most, LANES), F32),
@@ -365,6 +388,7 @@
             pltpu.SemaphoreType.DMA((7,)),
             pltpu.SemaphoreType.DMA((7,)),
             pltpu.SemaphoreType.DMA((2, 2 * len(counts))),
+            pltpu.SemaphoreType.DMA((2, splits, nh - 1)),
             *[
                 shape
                 for count in counts

time: 42.2 us -> 40.2 us (0.953)
  Pallas kernels: 40.5 us -> 39.5 us
  other arithmetic: 1.52 us -> 0.63 us
    pallas_call x1, Pallas kernels: 40.5 us -> 39.5 us  [on_device(): pl.pallas_call(functools.partial(kernel, (nh, nb, sub, cap)), out_shape=p...]
    convert_element_type x1, other arithmetic: 1.52 us -> 0.63 us  [on_device(): return pl.pallas_call(functools.partial(kernel, (nh, nb, sub, cap)), out_...]
where the time goes in v5:
time: 40.2 us; the launch traced here: 40.1 us
  Pallas kernels  39.5 us (98%)
  other arithmetic  0.63 us (2%)
    pallas_call x1, Pallas kernels, on_device(): pl.pallas_call(functools.partial(kernel, (nh, nb, sub, cap)), out_shape=p...  39.5 us

profile of v5, /device:TPU:0, one launch (start us, length us, event | category | flops | bytes accessed | tf_op | source)
XLA Modules:
  0.0 40.1 jit_solution(11736912607104165897)
XLA Ops:
  0.0 39.5 %layer.1 = f32[16,1536]{1,0:T(8,128)S(1)} custom-call(bf16[16,1536]{1,0:T(8,128)(2,1)} %q_hbm.1, bf16[16,1536]{1,0:T(8,128)(2,1)} %k_hbm.1, bf16[16,1536]{1,0:T(8,128)(2,1)} %v_hbm.1, bf16[16,1536]{1,0:T(8,128)(2,1)} %res_hbm.1, f32[1536]{0:T(1024)} %ag_hbm.1, f32[1536]{0:T(1024)} %shift_hbm.1, f32[1536]{0:T(1024)} %scale_hbm.1, f32[1536]{0:T(1024)} %eg_hbm.1, ...), custom_call_target="tpu_custom_call" | custom-call | tf_op jit(solution)/shard_map/layer/pallas_call | solution.py:363
  39.5 0.6 %convert_element_type.3 = bf16[16,1536]{1,0:T(8,128)(2,1)} convert(f32[16,1536]{1,0:T(8,128)S(1)} %layer.1) | non-fusion elementwise | flops 24576 | bytes 147456 | tf_op jit(solution)/shard_map/convert_element_type | solution.py:408

commit v6 on v5

--- a/solution.py
+++ b/solution.py
@@ -295,7 +295,7 @@
                 hidden[:, cols] = (0.5 * u * (1.0 + jnp.tanh(inner))).astype(BF16)
             return carry
 
-        lax.fori_loop(0, ff // up_tile, up_step, 0)
+        lax.fori_loop(0, ff // up_tile, up_step, 0, unroll=True)
 
     fetch[2].wait()
     for i, (start, stop) in enumerate(spans):

time: 40.2 us -> 39.3 us (0.978)
  Pallas kernels: 39.5 us -> 38.5 us
    pallas_call x1, Pallas kernels: 39.5 us -> 38.5 us  [on_device(): pl.pallas_call(functools.partial(kernel, (nh, nb, sub, cap)), out_shape=p...]
where the time goes in v6:
time: 39.3 us; the launch traced here: 39.2 us
  Pallas kernels  38.5 us (98%)
  other arithmetic  0.63 us (2%)
    pallas_call x1, Pallas kernels, on_device(): pl.pallas_call(functools.partial(kernel, (nh, nb, sub, cap)), out_shape=p...  38.5 us

profile of v6, /device:TPU:0, one launch (start us, length us, event | category | flops | bytes accessed | tf_op | source)
XLA Modules:
  0.0 39.2 jit_solution(12199349416512138356)
XLA Ops:
  0.0 38.5 %layer.1 = f32[16,1536]{1,0:T(8,128)S(1)} custom-call(bf16[16,1536]{1,0:T(8,128)(2,1)} %q_hbm.1, bf16[16,1536]{1,0:T(8,128)(2,1)} %k_hbm.1, bf16[16,1536]{1,0:T(8,128)(2,1)} %v_hbm.1, bf16[16,1536]{1,0:T(8,128)(2,1)} %res_hbm.1, f32[1536]{0:T(1024)} %ag_hbm.1, f32[1536]{0:T(1024)} %shift_hbm.1, f32[1536]{0:T(1024)} %scale_hbm.1, f32[1536]{0:T(1024)} %eg_hbm.1, ...), custom_call_target="tpu_custom_call" | custom-call | tf_op jit(solution)/shard_map/layer/pallas_call | solution.py:363
  38.5 0.6 %convert_element_type.3 = bf16[16,1536]{1,0:T(8,128)(2,1)} convert(f32[16,1536]{1,0:T(8,128)S(1)} %layer.1) | non-fusion elementwise | flops 24576 | bytes 147456 | tf_op jit(solution)/shard_map/convert_element_type | solution.py:408
